TPU v7x, 32 devices: a whole 2x2x4 slice. The times are simulated.
32 devices in a mesh: gx: 4 (over y, core), gy: 2 (over x), gz: 4 (over z).
Axes of the slice: x: 2, y: 2, z: 4, core: 2. Of those that a mesh axis runs over, the one named last changes fastest.
Arguments:
- stem: bfloat16 [2, 4, 2, 4, 256, 1024], P(None, 'gx', 'gy', 'gz'), may hold values from -6 to 6
- branch_one: bfloat16 [2, 2, 1024, 1024], replicated, may hold values from -0.125 to 0.125
- branch_two: bfloat16 [2, 2, 1024, 1024], P(None, None, ('gy', 'gz')), may hold values from -0.1875 to 0.1875
- branch_three: bfloat16 [2, 2, 1024, 1024], P(None, None, 'gz'), may hold values from -0.125 to 0.125
- slice_values: int32 [3], replicated, may hold values from 0 to 1, as said below
Outputs:
- contracted: bfloat16 [2, 4, 2, 4, 256, 1024], P(None, 'gx', 'gy', 'gz')
Inputs may be any that keep to these rules, and one draw needn't show every extreme that they name: `slice_values`: the first two slices differ.
All inputs are finite; a program needn't handle non-finite values.
Results may differ from a plain program's by a relative error of at most 0.0057.
Values may be sent and summed in bfloat16 or wider, within the bound.
A program may use at most 128 MiB of HBM per device.

v0:
```python
import jax
import jax.numpy as jnp
from jax import lax
from jax.sharding import PartitionSpec as P

WIDTH = 1024
ROWS = 256


def complex_matrix(branch):
    top_half = jnp.concatenate([branch[0], branch[1]], axis=1)
    bottom_half = jnp.concatenate([-branch[1], branch[0]], axis=1)
    return jnp.concatenate([top_half, bottom_half], axis=0)


def complex_product(operand, branch):
    joined = jnp.concatenate([operand[0], operand[1]], axis=1)
    result = jnp.dot(joined, complex_matrix(branch), preferred_element_type=jnp.float32)
    columns = branch.shape[2]
    return jnp.stack([result[:, :columns], result[:, columns:]])


def split_result(result):
    columns = result.shape[1] // 2
    return jnp.stack([result[:, :columns], result[:, columns:]])


def make_accumulate(operand, shard_rows):
    real_part = operand[0]
    imag_part = operand[1]
    joined = jnp.concatenate([real_part, imag_part], axis=1)
    return jnp.dot(joined, complex_matrix(shard_rows), preferred_element_type=jnp.float32)


def third_contraction(operand, branch_three, slice_values):
    local_third = lax.dynamic_index_in_dim(branch_three, slice_values[2], 0, keepdims=False)
    summed = make_accumulate(operand, lax.all_gather(local_third, "gz", axis=1, tiled=True))
    return split_result(summed).astype(jnp.bfloat16)


def body(stem, branch_one, branch_two, branch_three, slice_values):
    count_gx = lax.axis_size("gx")
    count_gy = lax.axis_size("gy")
    count_gz = lax.axis_size("gz")
    group_one = count_gx * count_gy
    group_two = count_gy * count_gz
    rows_one = ROWS // group_one
    rows_two = ROWS // group_two
    part_one = WIDTH // group_one
    part_two = WIDTH // group_two
    first_branch = lax.dynamic_index_in_dim(branch_one, slice_values[0], 0, keepdims=False)
    arrived = lax.all_to_all(
        stem.reshape(2, 1, group_one, rows_one, WIDTH),
        ("gx", "gy"),
        split_axis=2,
        concat_axis=1,
        tiled=True,
    )
    ordered = arrived.reshape(2, group_one, rows_one, part_one, group_one).transpose(0, 2, 4, 1, 3)
    ordered = ordered.reshape(2, ROWS, WIDTH)
    middle = complex_product(ordered, first_branch).astype(jnp.bfloat16)
    gathered = lax.all_to_all(
        middle.reshape(2, group_two, 1, rows_two, WIDTH),
        ("gy", "gz"),
        split_axis=1,
        concat_axis=2,
        tiled=True,
    )
    regrouped = gathered.reshape(2, group_two, rows_two, part_two, group_two).transpose(
        0, 2, 4, 1, 3
    )
    regrouped = regrouped.reshape(2, ROWS, WIDTH)
    local_second = lax.dynamic_index_in_dim(branch_two, slice_values[1], 0, keepdims=False)
    summed = make_accumulate(
        regrouped, lax.all_gather(local_second, ("gy", "gz"), axis=1, tiled=True)
    )
    second = split_result(summed).astype(jnp.bfloat16)
    returned = lax.all_to_all(
        second.reshape(2, 1, rows_two, group_two, group_two, part_two),
        ("gy", "gz"),
        split_axis=4,
        concat_axis=1,
        tiled=True,
    )
    result = third_contraction(returned.reshape(2, ROWS, WIDTH), branch_three, slice_values)
    return result.reshape(stem.shape)


def solution(mesh):
    return jax.shard_map(
        body,
        mesh=mesh,
        in_specs=(
            P(None, "gx", "gy", "gz", None, None),
            P(),
            P(None, None, ("gy", "gz"), None),
            P(None, None, "gz", None),
            P(),
        ),
        out_specs=P(None, "gx", "gy", "gz", None, None),
        check_vma=False,
    )
```

profile of v0, /device:TPU:0, one launch (start us, length us, event | category | flops | bytes accessed | tf_op | source)
XLA Modules:
  0.0 250.3 jit_solution(15021778729917147188)
XLA Ops:
  6.5 1.4 fusion.52
  9.9 1.9 constant_dynamic-slice_fusion.1
  13.0 5.2 %all-to-all-start = ((bf16[2,1,8,32,1024]{4,3,1,0,2:T(8,128)(2,1)}), bf16[2,1,8,32,1024]{4,3,1,0,2:T(8,128)(2,1)S(1)}, u32[]{:S(2)}, u32[]{:S(2)}) async-start(bf16[2,1,8,32,1024]{4,3,1,0,2:T(8,128)(2,1)} %copy.38), calls=%async_computation | async-start | bytes 2097152 | tf_op jit(solution)/shard_map/all_to_all | solution.py:52
  23.1 3.2 %dynamic-slice_bitcast_fusion.1 = bf16[1024,1024]{1,0:T(8,128)(2,1)} fusion(bf16[2,2,1024,1024]{3,2,1,0:T(8,128)(2,1)} %param.6, s32[]{:T(128)S(6)} %select_n.12), kind=kLoop, calls=%fused_computation.32 | loop fusion | bytes 4194308 | tf_op jit(solution)/shard_map/squeeze | solution.py:11
  26.3 3.8 %fusion.47 = (bf16[1024,1024]{1,0:T(8,128)(2,1)}, bf16[1024,1024]{1,0:T(8,128)(2,1)}) fusion(bf16[2,2,1024,1024]{3,2,1,0:T(8,128)(2,1)} %param.6, s32[]{:T(128)S(6)} %select_n.12, s32[]{:T(128)S(6)} %add.15), kind=kLoop, calls=%fused_computation.62 | loop fusion | flops 1048576 | bytes 6291464 | tf_op jit(solution)/shard_map/neg | solution.py:12
  30.1 8.6 %all-to-all-done = bf16[2,1,8,32,1024]{4,3,1,0,2:T(8,128)(2,1)S(1)} async-done(((bf16[2,1,8,32,1024]{4,3,1,0,2:T(8,128)(2,1)}), bf16[2,1,8,32,1024]{4,3,1,0,2:T(8,128)(2,1)S(1)}, u32[]{:S(2)}, u32[]{:S(2)}) %all-to-all-start) | async-done | bytes 1048608 | tf_op jit(solution)/shard_map/all_to_all | solution.py:52
  38.7 3.2 %copy.39 = bf16[2,1,8,32,1024]{3,4,2,0,1:T(8,128)(2,1)} copy(bf16[2,1,8,32,1024]{4,3,1,0,2:T(8,128)(2,1)S(1)} %all-to-all-done) | data formatting | bytes 2097152 | tf_op jit(solution)/shard_map/all_to_all | solution.py:52
  41.8 4.0 %fusion.49 = (bf16[1,32,8,8,128]{1,2,4,3,0:T(8,128)(2,1)}, bf16[1,32,8,8,128]{1,2,4,3,0:T(8,128)(2,1)S(1)}) fusion(bf16[2,32,8,8,128]{1,2,4,3,0:T(8,128)(2,1)} %bitcast.74), kind=kLoop, calls=%fused_computation.64 | loop fusion | bytes 2097152 | tf_op jit(solution)/shard_map/slice | solution.py:17
  45.8 3.5 %copy.40 = bf16[1,32,8,8,128]{4,3,2,1,0:T(8,128)(2,1)S(1)} copy(bf16[1,32,8,8,128]{1,2,4,3,0:T(8,128)(2,1)} %get-tuple-element.9) | data formatting | bytes 1048576 | tf_op jit(solution)/shard_map/slice | solution.py:17
  49.3 2.0 copy.41
  51.5 1.6 copy-done.4
  53.1 4.6 %fusion.30 = bf16[256,2048]{1,0:T(8,128)(2,1)S(1)} fusion(bf16[1024,1024]{1,0:T(8,128)(2,1)S(1)} %copy-done.4, bf16[1024,1024]{1,0:T(8,128)(2,1)} %get-tuple-element.5, bf16[1024,1024]{1,0:T(8,128)(2,1)} %get-tuple-element.6, bf16[256,1024]{1,0:T(8,128)(2,1)S(1)} %get-tuple-element.26, bf16[256,1024]{1,0:T(8,128)(2,1)S(1)} %get-tuple-element.27), kind=kOutput, calls=%fused_computation.26 | convolution fusion | flops 2183659520 | bytes 8388608 | tf_op jit(solution)/shard_map/dot_general | solution.py:18
  57.9 53.8 %all_to_all.33 = bf16[2,8,1,32,1024]{4,3,2,0,1:T(8,128)(2,1)S(1)} all-to-all(bf16[2,8,1,32,1024]{4,3,2,0,1:T(8,128)(2,1)S(1)} %pad_maximum_fusion), channel_id=1, replica_groups=mesh['gx'=4,'gy'=2,'gz'=4] {'gy','gz'}, dimensions={1} | all-to-all | bytes 2097152 | tf_op jit(solution)/shard_map/all_to_all | solution.py:62
  111.6 3.2 %copy.44 = bf16[2,8,1,32,1024]{3,4,1,0,2:T(8,128)(2,1)} copy(bf16[2,8,1,32,1024]{4,3,2,0,1:T(8,128)(2,1)S(1)} %all_to_all.33) | data formatting | bytes 2097152 | tf_op jit(solution)/shard_map/all_to_all | solution.py:62
  114.8 3.9 %fusion.48 = (bf16[1,32,8,8,128]{1,2,4,3,0:T(8,128)(2,1)S(1)}, bf16[1,32,8,8,128]{1,2,4,3,0:T(8,128)(2,1)}) fusion(bf16[2,32,8,8,128]{1,2,4,3,0:T(8,128)(2,1)} %bitcast.75), kind=kLoop, calls=%fused_computation.63 | loop fusion | bytes 2097152 | tf_op jit(solution)/shard_map/slice | solution.py:29
  118.7 3.7 %copy.46 = bf16[1,32,8,8,128]{4,3,2,1,0:T(8,128)(2,1)S(1)} copy(bf16[1,32,8,8,128]{1,2,4,3,0:T(8,128)(2,1)} %get-tuple-element.8) | data formatting | bytes 1048576 | tf_op jit(solution)/shard_map/slice | solution.py:30
  122.6 2.0 copy.45
  125.5 1.9 fusion.45
  129.4 2.4 fusion.27
  133.2 3.8 %all-to-all-start.2 = ((bf16[2,1,32,8,8,128]{5,3,2,0,1,4:T(8,128)(2,1)}), bf16[2,1,32,8,8,128]{5,3,2,0,1,4:T(8,128)(2,1)S(1)}, u32[]{:S(2)}, u32[]{:S(2)}) async-start(bf16[2,1,32,8,8,128]{5,3,2,0,1,4:T(8,128)(2,1)} %copy.49), calls=%async_computation.2 | async-start | bytes 2097152 | tf_op jit(solution)/shard_map/all_to_all | solution.py:78
  137.0 77.9 %all-gather.7.cloned.1.call-done = bf16[1,2,1024,1024]{3,2,1,0:T(8,128)(2,1)} async-done(((bf16[1,2,256,1024]{3,2,1,0:T(8,128)(2,1)}), bf16[1,2,1024,1024]{3,2,1,0:T(8,128)(2,1)}) %all-gather.7.cloned.1.call-update) | async-done | bytes 4194320 | tf_op jit(solution)/shard_map/all_gather | solution.py:37
  214.9 3.2 %fusion.46 = bf16[1024,1024]{1,0:T(8,128)(2,1)} fusion(bf16[1,2,1024,1024]{3,2,1,0:T(8,128)(2,1)} %all-gather.7.cloned.1.call-done), kind=kLoop, calls=%fused_computation.61 | loop fusion | flops 1048576 | bytes 4194304 | tf_op jit(solution)/shard_map/neg | solution.py:12
  218.1 2.4 slice_bitcast_fusion
  222.7 19.6 %fusion.24 = bf16[256,2048]{1,0:T(8,128)(2,1)S(1)} fusion(bf16[1024,1024]{1,0:T(8,128)(2,1)} %get-tuple-element.14, bf16[1024,1024]{1,0:T(8,128)(2,1)S(1)} %copy-done.5, bf16[1024,1024]{1,0:T(8,128)(2,1)S(1)} %copy-done.6, bf16[256,1024]{1,0:T(8,128)(2,1)S(1)} %bitcast.88, bf16[256,1024]{1,0:T(8,128)(2,1)S(1)} %bitcast.89), kind=kOutput, calls=%fused_computation.24 | convolution fusion | flops 2183659520 | bytes 8388608 | tf_op jit(solution)/shard_map/dot_general | solution.py:32
  (39 shorter events, 10.5 us)
Async XLA Ops:
  6.5 13.6 %copy-start = (bf16[2,2,256,1024]{3,2,1,0:T(8,128)(2,1)S(1)}, bf16[2,2,256,1024]{3,2,1,0:T(8,128)(2,1)}, u32[]{:S(2)}) copy-start(bf16[2,2,256,1024]{3,2,1,0:T(8,128)(2,1)} %param.8) | copy-start | bytes 6291460
  6.5 5.3 %copy-start.7 = (bf16[2,1,1,1,256,1024]{5,4,3,2,1,0:T(8,128)(2,1)S(1)}, bf16[2,1,1,1,256,1024]{5,4,3,2,1,0:T(8,128)(2,1)}, u32[]{:S(2)}) copy-start(bf16[2,1,1,1,256,1024]{5,4,3,2,1,0:T(8,128)(2,1)} %param.5) | copy-start | bytes 3145732
  6.5 119.0 %all-gather.5.cloned.1.call-start = ((), (), s32[]{:S(2)}) async-start(), calls=%async_computation.3 | async-start | bytes 4718592 | tf_op jit(solution)/shard_map/all_gather | solution.py:75
  13.0 25.7 %all-to-all-start = ((bf16[2,1,8,32,1024]{4,3,1,0,2:T(8,128)(2,1)}), bf16[2,1,8,32,1024]{4,3,1,0,2:T(8,128)(2,1)S(1)}, u32[]{:S(2)}, u32[]{:S(2)}) async-start(bf16[2,1,8,32,1024]{4,3,1,0,2:T(8,128)(2,1)} %copy.38), calls=%async_computation | async-start | bytes 2097152 | tf_op jit(solution)/shard_map/all_to_all | solution.py:52
  18.1 196.7 %all-gather.7.cloned.1.call-start = ((), (), s32[]{:S(2)}) async-start(), calls=%async_computation.4 | async-start | bytes 5242880 | tf_op jit(solution)/shard_map/all_gather | solution.py:37
  51.3 1.9 copy-start.4
  125.5 2.8 %copy-start.3 = (bf16[1,2,1024,1024]{3,2,1,0:T(8,128)(2,1)S(1)}, bf16[1,2,1024,1024]{3,2,1,0:T(8,128)(2,1)}, u32[]{:S(2)}) copy-start(bf16[1,2,1024,1024]{3,2,1,0:T(8,128)(2,1)} %all-gather.5.cloned.1.call-done) | copy-start | bytes 12582916
  128.4 1.0 copy-start.8
  133.2 87.3 %all-to-all-start.2 = ((bf16[2,1,32,8,8,128]{5,3,2,0,1,4:T(8,128)(2,1)}), bf16[2,1,32,8,8,128]{5,3,2,0,1,4:T(8,128)(2,1)S(1)}, u32[]{:S(2)}, u32[]{:S(2)}) async-start(bf16[2,1,32,8,8,128]{5,3,2,0,1,4:T(8,128)(2,1)} %copy.49), calls=%async_computation.2 | async-start | bytes 2097152 | tf_op jit(solution)/shard_map/all_to_all | solution.py:78
  214.9 3.2 %copy-start.2 = (bf16[1,2,1024,1024]{3,2,1,0:T(8,128)(2,1)S(1)}, bf16[1,2,1024,1024]{3,2,1,0:T(8,128)(2,1)}, u32[]{:S(2)}) copy-start(bf16[1,2,1024,1024]{3,2,1,0:T(8,128)(2,1)} %all-gather.7.cloned.1.call-done) | copy-start | bytes 12582916
  220.5 1.6 copy-start.5
  220.5 2.2 copy-start.6
  222.7 20.8 %copy-start.1 = (bf16[2,2,256,1024]{3,2,1,0:T(8,128)(2,1)S(1)}, bf16[2,2,256,1024]{3,2,1,0:T(8,128)(2,1)}, u32[]{:S(2)}) copy-start(bf16[2,2,256,1024]{3,2,1,0:T(8,128)(2,1)} %param.8) | copy-start | bytes 6291460
Sparse Core Ops, SparseCore 0:
  11.9 99.0 all-gather.4
  112.5 102.2 all-gather.6
where the time goes:
time: 251 us; the launch traced here: 250 us
  waiting for transfers between devices  86.5 us (34%)
  blocking collectives  53.8 us (21%)
  local copies, waits for them, and re-layouts  45.1 us (18%)
  matrix products  26.6 us (11%)
  between operations  19.3 us (8%)
  other arithmetic  10.2 us (4%)
  starting transfers between devices  8.99 us (4%)
    all_gather x1, waiting for transfers between devices, third_contraction(): lax.all_gather(local_third, 'gz', axis=1, tiled=True)  77.9 us
    all_to_all x1, blocking collectives, body(): lax.all_to_all(middle.reshape(2, group_two, 1, rows_two, WIDTH), ('gy', '...  53.8 us
    dot_general x2, matrix products, make_accumulate(): jnp.dot(joined, complex_matrix(shard_rows), preferred_element_type=jnp.fl...  22 us
    slice x3, local copies, waits for them, and re-layouts, complex_product(): joined = jnp.concatenate([operand[0], operand[1]], axis=1)  9.42 us
    neg x3, other arithmetic, complex_matrix(): bottom_half = jnp.concatenate([-branch[1], branch[0]], axis=1)  8.94 us
    all_to_all x1, waiting for transfers between devices, body(): lax.all_to_all(stem.reshape(2, 1, group_one, rows_one, WIDTH), ('gx', 'gy...  8.57 us
    unnamed x22, local copies, waits for them, and re-layouts  6.38 us
    squeeze x3, local copies, waits for them, and re-layouts, complex_matrix(): top_half = jnp.concatenate([branch[0], branch[1]], axis=1)  6.04 us
  transfers between devices with their start and end apart: 4, of which 2 were waited for; matrix products, arithmetic and copies ran while one was open for 21% of the time, Pallas kernels for 0%

commit v1 on v0

--- a/solution.py
+++ b/solution.py
@@ -5,6 +5,18 @@
 
 WIDTH = 1024
 ROWS = 256
+
+
+def collect(x, axis, dim):
+    ways, here, step = (lax.axis_size(axis), lax.axis_index(axis), x.shape[dim])
+    line, have = (x, 1)
+    while have < ways:
+        line = jnp.concatenate(
+            [line, lax.ppermute(line, axis, [(d, (d - have) % ways) for d in range(ways)])],
+            axis=dim,
+        )
+        have = 2 * have
+    return jnp.roll(line, here * step, axis=dim)
 
 
 def complex_matrix(branch):
@@ -34,7 +46,7 @@
 
 def third_contraction(operand, branch_three, slice_values):
     local_third = lax.dynamic_index_in_dim(branch_three, slice_values[2], 0, keepdims=False)
-    summed = make_accumulate(operand, lax.all_gather(local_third, "gz", axis=1, tiled=True))
+    summed = make_accumulate(operand, collect(local_third, "gz", 1))
     return split_result(summed).astype(jnp.bfloat16)
 
 

time: 251 us -> 294 us (1.17)
  waiting for transfers between devices: 86.5 us -> 155 us
  blocking collectives: 53.8 us -> 32.5 us
  matrix products: 26.6 us -> 7.18 us
  local copies, waits for them, and re-layouts: 45.1 us -> 58 us
  starting transfers between devices: 8.99 us -> 13.3 us
    ppermute x0 -> x2, waiting for transfers between devices: none -> 122 us  [collect(): lax.ppermute(line, axis, [(d, (d - have) % ways) for d in range(ways)])]
    all_gather x1 -> x0, waiting for transfers between devices: 77.9 us -> none  [third_contraction(): lax.all_gather(local_third, 'gz', axis=1, tiled=True)]
    all_to_all x1, waiting for transfers between devices: 0.01 us -> 22.1 us  [body(): lax.all_to_all(second.reshape(2, 1, rows_two, group_two, group_two, part_...]
    all_to_all x1, blocking collectives: 53.8 us -> 32.5 us  [body(): lax.all_to_all(middle.reshape(2, group_two, 1, rows_two, WIDTH), ('gy', '...]
    dot_general x2, matrix products: 22 us -> 4.79 us  [make_accumulate(): jnp.dot(joined, complex_matrix(shard_rows), preferred_element_type=jnp.fl...]
    unnamed x22 -> x27, local copies, waits for them, and re-layouts: 6.38 us -> 13.2 us
    ppermute x0 -> x2, starting transfers between devices: none -> 5.05 us  [collect(): lax.ppermute(line, axis, [(d, (d - have) % ways) for d in range(ways)])]
    squeeze x3, local copies, waits for them, and re-layouts: 6.04 us -> 9.25 us  [complex_matrix(): top_half = jnp.concatenate([branch[0], branch[1]], axis=1)]
  transfers between devices with their start and end apart: 4 -> 5, of which waited for: 2 -> 4; matrix products, arithmetic and copies ran while one was open for 21% -> 19% of each run, Pallas kernels for 0% -> 0%
where the time goes in v1:
time: 294 us
  waiting for transfers between devices  155 us (53%)
  local copies, waits for them, and re-layouts  58 us (20%)
  blocking collectives  32.5 us (11%)
  between operations  19.2 us (7%)
  starting transfers between devices  13.3 us (5%)
  other arithmetic  8.64 us (3%)
  matrix products  7.18 us (2%)
    ppermute x2, waiting for transfers between devices, collect(): lax.ppermute(line, axis, [(d, (d - have) % ways) for d in range(ways)])  122 us
    all_to_all x1, blocking collectives, body(): lax.all_to_all(middle.reshape(2, group_two, 1, rows_two, WIDTH), ('gy', '...  32.5 us
    all_to_all x1, waiting for transfers between devices, body(): lax.all_to_all(second.reshape(2, 1, rows_two, group_two, group_two, part_...  22.1 us
    unnamed x27, local copies, waits for them, and re-layouts  13.2 us
    slice x3, local copies, waits for them, and re-layouts, complex_product(): joined = jnp.concatenate([operand[0], operand[1]], axis=1)  11.6 us
    all_to_all x1, waiting for transfers between devices, body(): lax.all_to_all(stem.reshape(2, 1, group_one, rows_one, WIDTH), ('gx', 'gy...  10.1 us
    squeeze x3, local copies, waits for them, and re-layouts, complex_matrix(): top_half = jnp.concatenate([branch[0], branch[1]], axis=1)  9.25 us
    slice x3, local copies, waits for them, and re-layouts, make_accumulate(): real_part = operand[0]  5.98 us
  transfers between devices with their start and end apart: 5, of which 4 were waited for; matrix products, arithmetic and copies ran while one was open for 19% of the time, Pallas kernels for 0%

profile of v1, /device:TPU:0, one launch (start us, length us, event | category | flops | bytes accessed | tf_op | source)
XLA Modules:
  0.0 293.5 jit_solution(11697151875386247697)
XLA Ops:
  9.9 2.5 constant_dynamic-update-slice_fusion.5
  12.3 5.0 %collective-permute-start = (bf16[2,256,1024]{2,1,0:T(8,128)(2,1)S(1)}, bf16[2,256,1024]{2,1,0:T(8,128)(2,1)S(1)}, u32[]{:S(2)}, u32[]{:S(2)}) collective-permute-start(bf16[2,256,1024]{2,1,0:T(8,128)(2,1)S(1)} %get-tuple-element.10), channel_id=1, source_target_pairs={{0,3},{1,0},{2,1},{3,2},{4,7},{5,4},{6,5},{7,6},{8,11},{9,8},{10,9... | collective-permute-start | bytes 3145736 | tf_op jit(solution)/shard_map/ppermute | solution.py:15
  20.2 34.1 %collective-permute-done = bf16[2,256,1024]{2,1,0:T(8,128)(2,1)S(1)} collective-permute-done((bf16[2,256,1024]{2,1,0:T(8,128)(2,1)S(1)}, bf16[2,256,1024]{2,1,0:T(8,128)(2,1)S(1)}, u32[]{:S(2)}, u32[]{:S(2)}) %collective-permute-start) | collective-permute-done | bytes 1048608 | tf_op jit(solution)/shard_map/ppermute | solution.py:15
  56.8 4.7 %all-to-all-start = ((bf16[2,1,8,32,1024]{4,3,1,0,2:T(8,128)(2,1)}), bf16[2,1,8,32,1024]{4,3,1,0,2:T(8,128)(2,1)S(1)}, u32[]{:S(2)}, u32[]{:S(2)}) async-start(bf16[2,1,8,32,1024]{4,3,1,0,2:T(8,128)(2,1)} %copy.38), calls=%async_computation | async-start | bytes 2097152 | tf_op jit(solution)/shard_map/all_to_all | solution.py:64
  63.3 3.1 %dynamic-slice_bitcast_fusion.3 = bf16[1024,1024]{1,0:T(8,128)(2,1)} fusion(bf16[2,2,1024,1024]{3,2,1,0:T(8,128)(2,1)} %param.6, s32[]{:T(128)S(6)} %select_n.25), kind=kLoop, calls=%fused_computation.32 | loop fusion | bytes 4194308 | tf_op jit(solution)/shard_map/squeeze | solution.py:23
  66.4 10.1 %all-to-all-done = bf16[2,1,8,32,1024]{4,3,1,0,2:T(8,128)(2,1)S(1)} async-done(((bf16[2,1,8,32,1024]{4,3,1,0,2:T(8,128)(2,1)}), bf16[2,1,8,32,1024]{4,3,1,0,2:T(8,128)(2,1)S(1)}, u32[]{:S(2)}, u32[]{:S(2)}) %all-to-all-start) | async-done | bytes 1048608 | tf_op jit(solution)/shard_map/all_to_all | solution.py:64
  76.5 3.1 %copy.39 = bf16[2,1,8,32,1024]{3,4,2,0,1:T(8,128)(2,1)} copy(bf16[2,1,8,32,1024]{4,3,1,0,2:T(8,128)(2,1)S(1)} %all-to-all-done) | data formatting | bytes 2097152 | tf_op jit(solution)/shard_map/all_to_all | solution.py:64
  79.6 4.7 %fusion.49 = (bf16[1,32,8,8,128]{1,2,4,3,0:T(8,128)(2,1)}, bf16[1,32,8,8,128]{1,2,4,3,0:T(8,128)(2,1)}) fusion(bf16[2,32,8,8,128]{1,2,4,3,0:T(8,128)(2,1)} %bitcast.76), kind=kLoop, calls=%fused_computation.71 | loop fusion | bytes 2097152 | tf_op jit(solution)/shard_map/slice | solution.py:29
  84.3 3.5 %copy.41 = bf16[1,32,8,8,128]{4,3,2,1,0:T(8,128)(2,1)S(1)} copy(bf16[1,32,8,8,128]{1,2,4,3,0:T(8,128)(2,1)} %get-tuple-element.14) | data formatting | bytes 1048576 | tf_op jit(solution)/shard_map/slice | solution.py:29
  87.8 3.5 %copy.40 = bf16[1,32,8,8,128]{4,3,2,1,0:T(8,128)(2,1)S(1)} copy(bf16[1,32,8,8,128]{1,2,4,3,0:T(8,128)(2,1)} %get-tuple-element.13) | data formatting | bytes 1048576 | tf_op jit(solution)/shard_map/slice | solution.py:29
  92.5 88.4 %collective-permute-done.1 = bf16[2,512,1024]{2,1,0:T(8,128)(2,1)} collective-permute-done((bf16[2,512,1024]{2,1,0:T(8,128)(2,1)}, bf16[2,512,1024]{2,1,0:T(8,128)(2,1)}, u32[]{:S(2)}, u32[]{:S(2)}) %collective-permute-start.1) | collective-permute-done | bytes 2097184 | tf_op jit(solution)/shard_map/ppermute | solution.py:15
  180.9 3.1 %constant_dynamic-update-slice_fusion.3 = bf16[2,2048,1024]{2,1,0:T(8,128)(2,1)} fusion(bf16[2,2048,1024]{2,1,0:T(8,128)(2,1)} %constant_dynamic-update-slice_fusion.4, bf16[2,512,1024]{2,1,0:T(8,128)(2,1)} %collective-permute-done.1), kind=kLoop, calls=%fused_computation.60 | loop fusion | bytes 4194304
  186.1 3.2 %constant_dynamic-update-slice_fusion = bf16[2,2048,1024]{2,1,0:T(8,128)(2,1)} fusion(bf16[2,2048,1024]{2,1,0:T(8,128)(2,1)} %constant_dynamic-update-slice_fusion.1, bf16[2,512,1024]{2,1,0:T(8,128)(2,1)} %collective-permute-done.1), kind=kLoop, calls=%fused_computation.57 | loop fusion | bytes 4194304 | tf_op jit(solution)/shard_map/jit(_roll_dynamic)/concatenate | solution.py:19
  189.3 5.7 %fusion.46 = (bf16[1024,1024]{1,0:T(8,128)(2,1)S(1)}, bf16[1024,1024]{1,0:T(8,128)(2,1)S(1)}, bf16[1024,1024]{1,0:T(8,128)(2,1)}, bf16[1024,1024]{1,0:T(8,128)(2,1)}) fusion(bf16[2,2,1024,1024]{3,2,1,0:T(8,128)(2,1)} %param.6, s32[]{:T(128)S(6)} %select_n.25, s32[]{:T(128)S(6)} %add.27, bf16[2,2048,1024]{2,1,0:T(8,128)(2,1)} %constant_dynamic-update-slice_fusion, ...), kind=kLoop, calls=%fused_computation.68 | loop fusion | flops 6291456 | bytes 12582924 | tf_op jit(solution)/shard_map/neg | solution.py:24
  197.6 32.5 %all_to_all.33 = bf16[2,8,1,32,1024]{4,3,2,0,1:T(8,128)(2,1)S(1)} all-to-all(bf16[2,8,1,32,1024]{4,3,2,0,1:T(8,128)(2,1)S(1)} %pad_maximum_fusion.1), channel_id=1, replica_groups=mesh['gx'=4,'gy'=2,'gz'=4] {'gy','gz'}, dimensions={1} | all-to-all | bytes 2097152 | tf_op jit(solution)/shard_map/all_to_all | solution.py:74
  230.0 3.1 %copy.44 = bf16[2,8,1,32,1024]{3,4,1,0,2:T(8,128)(2,1)} copy(bf16[2,8,1,32,1024]{4,3,2,0,1:T(8,128)(2,1)S(1)} %all_to_all.33) | data formatting | bytes 2097152 | tf_op jit(solution)/shard_map/all_to_all | solution.py:74
  233.2 3.9 %fusion.48 = (bf16[1,32,8,8,128]{1,2,4,3,0:T(8,128)(2,1)S(1)}, bf16[1,32,8,8,128]{1,2,4,3,0:T(8,128)(2,1)}) fusion(bf16[2,32,8,8,128]{1,2,4,3,0:T(8,128)(2,1)} %bitcast.77), kind=kLoop, calls=%fused_computation.70 | loop fusion | bytes 2097152 | tf_op jit(solution)/shard_map/slice | solution.py:41
  237.1 3.5 %copy.46 = bf16[1,32,8,8,128]{4,3,2,1,0:T(8,128)(2,1)S(1)} copy(bf16[1,32,8,8,128]{1,2,4,3,0:T(8,128)(2,1)} %get-tuple-element.12) | data formatting | bytes 1048576 | tf_op jit(solution)/shard_map/slice | solution.py:42
  243.6 2.8 slice_bitcast_fusion
  248.1 2.4 fusion.27
  251.9 3.6 %all-to-all-start.2 = ((bf16[2,1,32,8,8,128]{5,3,2,0,1,4:T(8,128)(2,1)}), bf16[2,1,32,8,8,128]{5,3,2,0,1,4:T(8,128)(2,1)S(1)}, u32[]{:S(2)}, u32[]{:S(2)}) async-start(bf16[2,1,32,8,8,128]{5,3,2,0,1,4:T(8,128)(2,1)} %copy.49), calls=%async_computation.2 | async-start | bytes 2097152 | tf_op jit(solution)/shard_map/all_to_all | solution.py:90
  255.5 3.3 %dynamic-slice_bitcast_fusion.1 = bf16[1024,1024]{1,0:T(8,128)(2,1)} fusion(bf16[2,2048,1024]{2,1,0:T(8,128)(2,1)} %constant_dynamic-update-slice_fusion, s32[]{:T(128)S(6)} %select_n.29), kind=kLoop, calls=%fused_computation.28 | loop fusion | bytes 4194308 | tf_op jit(solution)/shard_map/squeeze | solution.py:23
  258.8 22.1 %all-to-all-done.2 = bf16[2,1,32,8,8,128]{5,3,2,0,1,4:T(8,128)(2,1)S(1)} async-done(((bf16[2,1,32,8,8,128]{5,3,2,0,1,4:T(8,128)(2,1)}), bf16[2,1,32,8,8,128]{5,3,2,0,1,4:T(8,128)(2,1)S(1)}, u32[]{:S(2)}, u32[]{:S(2)}) %all-to-all-start.2) | async-done | bytes 1048608 | tf_op jit(solution)/shard_map/all_to_all | solution.py:90
  283.2 2.4 fusion.24
  (45 shorter events, 20.1 us)
Async XLA Ops:
  6.5 12.8 %copy-start = (bf16[2,2,128,1024]{3,2,1,0:T(8,128)(2,1)S(1)}, bf16[2,2,128,1024]{3,2,1,0:T(8,128)(2,1)}, u32[]{:S(2)}) copy-start(bf16[2,2,128,1024]{3,2,1,0:T(8,128)(2,1)} %param.7) | copy-start | bytes 3145732
  6.5 237.0 %all-gather.3.cloned.1.call-start = ((), (), s32[]{:S(2)}) async-start(), calls=%async_computation.3 | async-start | bytes 4718592 | tf_op jit(solution)/shard_map/all_gather | solution.py:87
  12.3 41.9 %collective-permute-start = (bf16[2,256,1024]{2,1,0:T(8,128)(2,1)S(1)}, bf16[2,256,1024]{2,1,0:T(8,128)(2,1)S(1)}, u32[]{:S(2)}, u32[]{:S(2)}) collective-permute-start(bf16[2,256,1024]{2,1,0:T(8,128)(2,1)S(1)} %get-tuple-element.10), channel_id=1, source_target_pairs={{0,3},{1,0},{2,1},{3,2},{4,7},{5,4},{6,5},{7,6},{8,11},{9,8},{10,9... | collective-permute-start | bytes 3145736 | tf_op jit(solution)/shard_map/ppermute | solution.py:15
  20.2 35.6 %copy-start.7 = (bf16[2,1,1,1,256,1024]{5,4,3,2,1,0:T(8,128)(2,1)S(1)}, bf16[2,1,1,1,256,1024]{5,4,3,2,1,0:T(8,128)(2,1)}, u32[]{:S(2)}) copy-start(bf16[2,1,1,1,256,1024]{5,4,3,2,1,0:T(8,128)(2,1)} %param.5) | copy-start | bytes 3145732
  55.8 125.2 %collective-permute-start.1 = (bf16[2,512,1024]{2,1,0:T(8,128)(2,1)}, bf16[2,512,1024]{2,1,0:T(8,128)(2,1)}, u32[]{:S(2)}, u32[]{:S(2)}) collective-permute-start(bf16[2,512,1024]{2,1,0:T(8,128)(2,1)} %pad_maximum_fusion), channel_id=1, source_target_pairs={{0,2},{1,3},{2,0},{3,1},{4,6},{5,7},{6,4},{7,5},{8,10},{9,11},{10,... | collective-permute-start | bytes 6291464 | tf_op jit(solution)/shard_map/ppermute | solution.py:15
  56.8 19.7 %all-to-all-start = ((bf16[2,1,8,32,1024]{4,3,1,0,2:T(8,128)(2,1)}), bf16[2,1,8,32,1024]{4,3,1,0,2:T(8,128)(2,1)S(1)}, u32[]{:S(2)}, u32[]{:S(2)}) async-start(bf16[2,1,8,32,1024]{4,3,1,0,2:T(8,128)(2,1)} %copy.38), calls=%async_computation | async-start | bytes 2097152 | tf_op jit(solution)/shard_map/all_to_all | solution.py:64
  189.3 5.7 %copy-start.5 = (bf16[1024,1024]{1,0:T(8,128)(2,1)S(1)}, bf16[1024,1024]{1,0:T(8,128)(2,1)}, u32[]{:S(2)}) copy-start(bf16[1024,1024]{1,0:T(8,128)(2,1)} %dynamic-slice_bitcast_fusion.3) | copy-start | bytes 6291460
  243.6 3.5 %copy-start.2 = (bf16[1,2,1024,1024]{3,2,1,0:T(8,128)(2,1)S(1)}, bf16[1,2,1024,1024]{3,2,1,0:T(8,128)(2,1)}, u32[]{:S(2)}) copy-start(bf16[1,2,1024,1024]{3,2,1,0:T(8,128)(2,1)} %all-gather.3.cloned.1.call-done) | copy-start | bytes 12582916
  247.0 1.0 copy-start.8
  251.9 29.0 %all-to-all-start.2 = ((bf16[2,1,32,8,8,128]{5,3,2,0,1,4:T(8,128)(2,1)}), bf16[2,1,32,8,8,128]{5,3,2,0,1,4:T(8,128)(2,1)S(1)}, u32[]{:S(2)}, u32[]{:S(2)}) async-start(bf16[2,1,32,8,8,128]{5,3,2,0,1,4:T(8,128)(2,1)} %copy.49), calls=%async_computation.2 | async-start | bytes 2097152 | tf_op jit(solution)/shard_map/all_to_all | solution.py:90
  255.5 25.7 %copy-start.3 = (bf16[1024,1024]{1,0:T(8,128)(2,1)S(1)}, bf16[1024,1024]{1,0:T(8,128)(2,1)}, u32[]{:S(2)}) copy-start(bf16[1024,1024]{1,0:T(8,128)(2,1)} %get-tuple-element.28) | copy-start | bytes 6291460
  280.9 1.6 copy-start.4
  280.9 2.2 copy-start.6
  283.1 3.5 %copy-start.1 = (bf16[2,2,128,1024]{3,2,1,0:T(8,128)(2,1)S(1)}, bf16[2,2,128,1024]{3,2,1,0:T(8,128)(2,1)}, u32[]{:S(2)}) copy-start(bf16[2,2,128,1024]{3,2,1,0:T(8,128)(2,1)} %param.7) | copy-start | bytes 3145732
Sparse Core Ops, SparseCore 0:
  20.3 144.4 all-gather.2
